TPU v7x, 512 devices: a whole 4x8x8 slice. The times are simulated.
512 devices in a mesh: vol: 64 (over z_lo, y, core), strip: 8 (over z_hi, x).
Axes of the slice: x: 4, y: 8, z: 8 (z_hi: 2, z_lo: 4; z = z_hi * 4 + z_lo), core: 2. Of those that a mesh axis runs over, the one named last changes fastest.
Arguments:
- frames: bfloat16 [128, 1, 2048, 1024], P('vol', None, 'strip'), may hold values from 0.5 to 4
- kappa: float32 [128], P('vol'), may hold values from 0.3 to 3
Outputs:
- dff: bfloat16 [128, 1, 256, 8, 1024], P(None, None, 'vol', 'strip')
- slope: bfloat16 [128, 1, 256, 8, 1024], P(None, None, 'vol', 'strip')
All inputs are finite; a program needn't handle non-finite values.
Results may differ from a plain program's by a relative error of at most 0.0097.
Values may be sent and summed in bfloat16 or wider, within the bound.
No kernel may reach another device: no remote copies, remote signals or barrier semaphores. Data moves between devices by JAX's collectives and lax.ppermute only.
A program may use at most 64 MiB of HBM per device.

v0:
```python
import jax
import jax.numpy as jnp
from jax import lax
from jax.sharding import PartitionSpec as P

PASSES = 3
BAND = 16


def extended_2(value, sides, width):
    for axis, dim in sides:
        devices, length = (lax.axis_size(axis), value.shape[dim])
        up = [(i, (i + 1) % devices) for i in range(devices - 1)]
        down = [(j, i) for i, j in up]
        last = lax.slice_in_dim(value, length - width, length, axis=dim)
        first = lax.slice_in_dim(value, 0, width, axis=dim)
        before = lax.ppermute(last, axis, up)
        after = lax.ppermute(first, axis, down)
        value = jnp.concatenate([before, value, after], axis=dim)
    return value


def flux(diff, kap):
    ratio = diff / kap
    return diff / (1.0 + ratio * ratio)


def advance(extended, kap):
    center = extended[..., 1:-1, :]
    upper = extended[..., :-2, :] - center
    lower = extended[..., 2:, :] - center
    padded = jnp.pad(center, [(0, 0)] * (center.ndim - 1) + [(1, 1)])
    left = padded[..., :-2] - center
    right = padded[..., 2:] - center
    total = flux(upper, kap) + flux(lower, kap) + flux(left, kap) + flux(right, kap)
    return center + 0.2 * total


def smooth_weights(times):
    steps = jnp.arange(times, dtype=jnp.int32)
    gap = jnp.abs(steps[:, None] - steps[None, :])
    raw = jnp.where(gap <= BAND, BAND + 1 - gap, 0).astype(jnp.float32)
    return (raw / jnp.sum(raw, axis=1, keepdims=True)).astype(jnp.bfloat16)


def detrend(piece):
    times = piece.shape[0]
    weights = smooth_weights(times)
    flat = piece.reshape(times, -1)
    baseline = jnp.dot(weights, flat, preferred_element_type=jnp.float32)
    ratio = (flat.astype(jnp.float32) - baseline) / (baseline + 0.1)
    slope = jnp.concatenate(
        [ratio[1:2] - ratio[0:1], (ratio[2:] - ratio[:-2]) * 0.5, ratio[-1:] - ratio[-2:-1]], axis=0
    )
    return (
        ratio.reshape(piece.shape).astype(jnp.bfloat16),
        slope.reshape(piece.shape).astype(jnp.bfloat16),
    )


def local(frames, kappa):
    kap = kappa[:, None, None, None]
    field = frames.astype(jnp.float32)
    for step in range(PASSES):
        extended = extended_2(field, (("strip", 2),), 1)
        field = advance(extended, kap)
    stored = field.astype(jnp.bfloat16)
    ratio, slope = detrend(lax.all_to_all(stored, "vol", split_axis=2, concat_axis=0, tiled=True))
    return (ratio[:, :, :, None, :], slope[:, :, :, None, :])


def solution(mesh):
    placed = (P("vol", None, "strip", None), P("vol"))
    return jax.shard_map(
        local,
        mesh=mesh,
        in_specs=placed,
        out_specs=(P(None, None, "vol", "strip", None), P(None, None, "vol", "strip", None)),
        check_vma=False,
    )
```

profile of v0, /device:TPU:7, one launch (start us, length us, event | category | flops | bytes accessed | tf_op | source)
XLA Modules:
  0.0 106.4 jit_solution(1144931617588871949)
XLA Ops:
  0.6 0.0 copy-start
  0.6 0.0 copy-start.1
  0.7 0.9 fusion.23
  1.5 10.6 %collective-permute-start = (f32[2,1,1,1024]{3,2,1,0:T(1,128)S(1)}, f32[2,1,1,1024]{3,2,1,0:T(1,128)S(1)}, u32[]{:S(2)}, u32[]{:S(2)}) collective-permute-start(f32[2,1,1,1024]{3,2,1,0:T(1,128)S(1)} %get-tuple-element.20), channel_id=1, source_target_pairs={{0,1},{1,2},{2,3},{3,4},{4,5},{5,6},{6,7},{8,9},{9,10},{10,11},{11... | collective-permute-start | bytes 24584 | tf_op jit(solution)/shard_map/ppermute | solution.py:17
  12.1 1.9 %collective-permute-start.1 = (f32[2,1,1,1024]{3,2,1,0:T(1,128)S(1)}, f32[2,1,1,1024]{3,2,1,0:T(1,128)S(1)}, u32[]{:S(2)}, u32[]{:S(2)}) collective-permute-start(f32[2,1,1,1024]{3,2,1,0:T(1,128)S(1)} %get-tuple-element.21), channel_id=1, source_target_pairs={{1,0},{2,1},{3,2},{4,3},{5,4},{6,5},{7,6},{9,8},{10,9},{11,10},{12... | collective-permute-start | bytes 24584 | tf_op jit(solution)/shard_map/ppermute | solution.py:18
  14.0 1.5 %convert_element_type.49 = f32[2,1,256,1024]{3,2,1,0:T(8,128)S(1)} convert(bf16[2,1,256,1024]{3,2,1,0:T(8,128)(2,1)} %param.2) | non-fusion elementwise | flops 524288 | bytes 3145728 | tf_op jit(solution)/shard_map/convert_element_type | solution.py:63
  15.5 0.0 collective-permute-done
  15.5 7.0 %collective-permute-done.1 = f32[2,1,1,1024]{3,2,1,0:T(1,128)S(1)} collective-permute-done((f32[2,1,1,1024]{3,2,1,0:T(1,128)S(1)}, f32[2,1,1,1024]{3,2,1,0:T(1,128)S(1)}, u32[]{:S(2)}, u32[]{:S(2)}) %collective-permute-start.1) | collective-permute-done | bytes 8224 | tf_op jit(solution)/shard_map/ppermute | solution.py:18
  22.5 0.0 copy-done
  22.5 0.0 copy-done.1
  22.5 2.7 %convert_add_fusion = f32[2,1,256,1024]{3,2,1,0:T(8,128)S(1)} fusion(bf16[2,1,256,1024]{3,2,1,0:T(8,128)(2,1)S(1)} %copy-done, f32[2,1,256,1024]{3,2,1,0:T(8,128)S(1)} %convert_element_type.49, f32[2,1,1,1024]{3,2,1,0:T(1,128)S(1)} %collective-permute-done.1, f32[2,1,1,1024]{3,2,1,0:T(1,128)S(1)} %collective-permute-done, f32[2]{0:T(128)S(1)} %copy-done.1), kind=kLoop, calls=%fused_computation | loop fusion | flops 14680064 | bytes 5259272 | tf_op jit(solution)/shard_map/add | solution.py:36
  25.2 2.4 %collective-permute-start.2 = (f32[2,1,1,1024]{3,2,1,0:T(1,128)S(1)}, f32[2,1,1,1024]{3,2,1,0:T(1,128)S(1)}, u32[]{:S(2)}, u32[]{:S(2)}) collective-permute-start(f32[2,1,1,1024]{3,2,1,0:T(1,128)S(1)} %get-tuple-element.18), channel_id=1, source_target_pairs={{0,1},{1,2},{2,3},{3,4},{4,5},{5,6},{6,7},{8,9},{9,10},{10,11},{11... | collective-permute-start | bytes 24584 | tf_op jit(solution)/shard_map/ppermute | solution.py:17
  27.7 2.9 %collective-permute-start.3 = (f32[2,1,1,1024]{3,2,1,0:T(1,128)S(1)}, f32[2,1,1,1024]{3,2,1,0:T(1,128)S(1)}, u32[]{:S(2)}, u32[]{:S(2)}) collective-permute-start(f32[2,1,1,1024]{3,2,1,0:T(1,128)S(1)} %get-tuple-element.19), channel_id=1, source_target_pairs={{1,0},{2,1},{3,2},{4,3},{5,4},{6,5},{7,6},{9,8},{10,9},{11,10},{12... | collective-permute-start | bytes 24584 | tf_op jit(solution)/shard_map/ppermute | solution.py:18
  30.5 0.0 collective-permute-done.2
  30.5 7.5 %collective-permute-done.3 = f32[2,1,1,1024]{3,2,1,0:T(1,128)S(1)} collective-permute-done((f32[2,1,1,1024]{3,2,1,0:T(1,128)S(1)}, f32[2,1,1,1024]{3,2,1,0:T(1,128)S(1)}, u32[]{:S(2)}, u32[]{:S(2)}) %collective-permute-start.3) | collective-permute-done | bytes 8224 | tf_op jit(solution)/shard_map/ppermute | solution.py:18
  38.1 2.6 %multiply_add_fusion = f32[2,1,256,1024]{3,2,1,0:T(8,128)S(1)} fusion(f32[2,1,256,1024]{3,2,1,0:T(8,128)S(1)} %convert_add_fusion, f32[2,1,1,1024]{3,2,1,0:T(1,128)S(1)} %collective-permute-done.3, f32[2,1,1,1024]{3,2,1,0:T(1,128)S(1)} %collective-permute-done.2, f32[2]{0:T(128)S(1)} %copy-done.1), kind=kLoop, calls=%fused_computation.30 | loop fusion | flops 14155776 | bytes 4210696 | tf_op jit(solution)/shard_map/add | solution.py:36
  40.7 1.9 %collective-permute-start.4 = (f32[2,1,1,1024]{3,2,1,0:T(1,128)S(1)}, f32[2,1,1,1024]{3,2,1,0:T(1,128)S(1)}, u32[]{:S(2)}, u32[]{:S(2)}) collective-permute-start(f32[2,1,1,1024]{3,2,1,0:T(1,128)S(1)} %get-tuple-element.16), channel_id=1, source_target_pairs={{0,1},{1,2},{2,3},{3,4},{4,5},{5,6},{6,7},{8,9},{9,10},{10,11},{11... | collective-permute-start | bytes 24584 | tf_op jit(solution)/shard_map/ppermute | solution.py:17
  42.7 3.4 %collective-permute-start.5 = (f32[2,1,1,1024]{3,2,1,0:T(1,128)S(1)}, f32[2,1,1,1024]{3,2,1,0:T(1,128)S(1)}, u32[]{:S(2)}, u32[]{:S(2)}) collective-permute-start(f32[2,1,1,1024]{3,2,1,0:T(1,128)S(1)} %get-tuple-element.17), channel_id=1, source_target_pairs={{1,0},{2,1},{3,2},{4,3},{5,4},{6,5},{7,6},{9,8},{10,9},{11,10},{12... | collective-permute-start | bytes 24584 | tf_op jit(solution)/shard_map/ppermute | solution.py:18
  46.0 0.0 collective-permute-done.4
  46.1 7.0 %collective-permute-done.5 = f32[2,1,1,1024]{3,2,1,0:T(1,128)S(1)} collective-permute-done((f32[2,1,1,1024]{3,2,1,0:T(1,128)S(1)}, f32[2,1,1,1024]{3,2,1,0:T(1,128)S(1)}, u32[]{:S(2)}, u32[]{:S(2)}) %collective-permute-start.5) | collective-permute-done | bytes 8224 | tf_op jit(solution)/shard_map/ppermute | solution.py:18
  53.1 2.7 %add_convert_fusion = bf16[2,1,256,1024]{3,2,1,0:T(8,128)(2,1)S(1)} fusion(f32[2,1,256,1024]{3,2,1,0:T(8,128)S(1)} %multiply_add_fusion, f32[2,1,1,1024]{3,2,1,0:T(1,128)S(1)} %collective-permute-done.5, f32[2,1,1,1024]{3,2,1,0:T(1,128)S(1)} %collective-permute-done.4, f32[2]{0:T(128)S(1)} %copy-done.1), kind=kLoop, calls=%fused_computation.29 | loop fusion | flops 14680064 | bytes 3162120 | tf_op jit(solution)/shard_map/convert_element_type | solution.py:67
  55.8 2.0 %copy.41 = bf16[2,1,256,1024]{3,0,1,2:T(2,128)(2,1)} copy(bf16[2,1,256,1024]{3,2,1,0:T(8,128)(2,1)S(1)} %add_convert_fusion) | data formatting | bytes 2097152 | tf_op jit(solution)/shard_map/convert_element_type | solution.py:67
  57.8 14.3 %all-to-all-start = ((bf16[2,1,256,1024]{3,0,1,2:T(2,128)(2,1)}), bf16[2,1,256,1024]{3,0,1,2:T(2,128)(2,1)S(1)}, u32[]{:S(2)}, u32[]{:S(2)}) async-start(bf16[2,1,256,1024]{3,0,1,2:T(2,128)(2,1)} %copy.41), calls=%async_computation | async-start | bytes 2097152 | tf_op jit(solution)/shard_map/all_to_all | solution.py:68
  72.1 0.1 convert_reduce_fusion
  72.3 28.7 %all-to-all-done = bf16[2,1,256,1024]{3,0,1,2:T(2,128)(2,1)S(1)} async-done(((bf16[2,1,256,1024]{3,0,1,2:T(2,128)(2,1)}), bf16[2,1,256,1024]{3,0,1,2:T(2,128)(2,1)S(1)}, u32[]{:S(2)}, u32[]{:S(2)}) %all-to-all-start) | async-done | bytes 1048608 | tf_op jit(solution)/shard_map/all_to_all | solution.py:68
  101.0 0.5 copy.42
  101.5 0.4 copy.45
  101.9 0.7 fusion.24
  102.6 0.3 fusion.5
  102.9 1.6 %convert_element_type.55 = bf16[128,1,4,1,1024]{4,2,0,3,1:T(4,128)(2,1)} reshape(bf16[128,4096]{1,0:T(8,128)(2,1)S(1)} %get-tuple-element.22) | data formatting | bytes 2097152 | tf_op jit(solution)/shard_map/convert_element_type | solution.py:56
  104.5 0.3 pad_maximum_fusion.6
  104.8 1.6 %convert_element_type.56 = bf16[128,1,4,1,1024]{4,2,0,3,1:T(4,128)(2,1)} reshape(bf16[128,4096]{1,0:T(8,128)(2,1)S(1)} %pad_maximum_fusion.6) | data formatting | bytes 2097152 | tf_op jit(solution)/shard_map/convert_element_type | solution.py:57
  (3 shorter events, 0.1 us)
Async XLA Ops:
  0.6 21.9 %copy-start = (bf16[2,1,256,1024]{3,2,1,0:T(8,128)(2,1)S(1)}, bf16[2,1,256,1024]{3,2,1,0:T(8,128)(2,1)}, u32[]{:S(2)}) copy-start(bf16[2,1,256,1024]{3,2,1,0:T(8,128)(2,1)} %param.2) | copy-start | bytes 3145732
  0.6 21.9 %copy-start.1 = (f32[2]{0:T(128)S(1)}, f32[2]{0:T(128)}, u32[]{:S(2)}) copy-start(f32[2]{0:T(128)} %param.3) | copy-start | bytes 28
  1.5 14.0 %collective-permute-start = (f32[2,1,1,1024]{3,2,1,0:T(1,128)S(1)}, f32[2,1,1,1024]{3,2,1,0:T(1,128)S(1)}, u32[]{:S(2)}, u32[]{:S(2)}) collective-permute-start(f32[2,1,1,1024]{3,2,1,0:T(1,128)S(1)} %get-tuple-element.20), channel_id=1, source_target_pairs={{0,1},{1,2},{2,3},{3,4},{4,5},{5,6},{6,7},{8,9},{9,10},{10,11},{11... | collective-permute-start | bytes 24584 | tf_op jit(solution)/shard_map/ppermute | solution.py:17
  12.1 10.4 %collective-permute-start.1 = (f32[2,1,1,1024]{3,2,1,0:T(1,128)S(1)}, f32[2,1,1,1024]{3,2,1,0:T(1,128)S(1)}, u32[]{:S(2)}, u32[]{:S(2)}) collective-permute-start(f32[2,1,1,1024]{3,2,1,0:T(1,128)S(1)} %get-tuple-element.21), channel_id=1, source_target_pairs={{1,0},{2,1},{3,2},{4,3},{5,4},{6,5},{7,6},{9,8},{10,9},{11,10},{12... | collective-permute-start | bytes 24584 | tf_op jit(solution)/shard_map/ppermute | solution.py:18
  25.2 5.3 %collective-permute-start.2 = (f32[2,1,1,1024]{3,2,1,0:T(1,128)S(1)}, f32[2,1,1,1024]{3,2,1,0:T(1,128)S(1)}, u32[]{:S(2)}, u32[]{:S(2)}) collective-permute-start(f32[2,1,1,1024]{3,2,1,0:T(1,128)S(1)} %get-tuple-element.18), channel_id=1, source_target_pairs={{0,1},{1,2},{2,3},{3,4},{4,5},{5,6},{6,7},{8,9},{9,10},{10,11},{11... | collective-permute-start | bytes 24584 | tf_op jit(solution)/shard_map/ppermute | solution.py:17
  27.7 10.4 %collective-permute-start.3 = (f32[2,1,1,1024]{3,2,1,0:T(1,128)S(1)}, f32[2,1,1,1024]{3,2,1,0:T(1,128)S(1)}, u32[]{:S(2)}, u32[]{:S(2)}) collective-permute-start(f32[2,1,1,1024]{3,2,1,0:T(1,128)S(1)} %get-tuple-element.19), channel_id=1, source_target_pairs={{1,0},{2,1},{3,2},{4,3},{5,4},{6,5},{7,6},{9,8},{10,9},{11,10},{12... | collective-permute-start | bytes 24584 | tf_op jit(solution)/shard_map/ppermute | solution.py:18
  40.7 5.3 %collective-permute-start.4 = (f32[2,1,1,1024]{3,2,1,0:T(1,128)S(1)}, f32[2,1,1,1024]{3,2,1,0:T(1,128)S(1)}, u32[]{:S(2)}, u32[]{:S(2)}) collective-permute-start(f32[2,1,1,1024]{3,2,1,0:T(1,128)S(1)} %get-tuple-element.16), channel_id=1, source_target_pairs={{0,1},{1,2},{2,3},{3,4},{4,5},{5,6},{6,7},{8,9},{9,10},{10,11},{11... | collective-permute-start | bytes 24584 | tf_op jit(solution)/shard_map/ppermute | solution.py:17
  42.7 10.4 %collective-permute-start.5 = (f32[2,1,1,1024]{3,2,1,0:T(1,128)S(1)}, f32[2,1,1,1024]{3,2,1,0:T(1,128)S(1)}, u32[]{:S(2)}, u32[]{:S(2)}) collective-permute-start(f32[2,1,1,1024]{3,2,1,0:T(1,128)S(1)} %get-tuple-element.17), channel_id=1, source_target_pairs={{1,0},{2,1},{3,2},{4,3},{5,4},{6,5},{7,6},{9,8},{10,9},{11,10},{12... | collective-permute-start | bytes 24584 | tf_op jit(solution)/shard_map/ppermute | solution.py:18
  57.8 43.1 %all-to-all-start = ((bf16[2,1,256,1024]{3,0,1,2:T(2,128)(2,1)}), bf16[2,1,256,1024]{3,0,1,2:T(2,128)(2,1)S(1)}, u32[]{:S(2)}, u32[]{:S(2)}) async-start(bf16[2,1,256,1024]{3,0,1,2:T(2,128)(2,1)} %copy.41), calls=%async_computation | async-start | bytes 2097152 | tf_op jit(solution)/shard_map/all_to_all | solution.py:68
where the time goes:
time: 107 us; the launch traced here: 106 us
  waiting for transfers between devices  50.3 us (47%)
  starting transfers between devices  37.3 us (35%)
  other arithmetic  10.3 us (10%)
  local copies, waits for them, and re-layouts  7.04 us (7%)
    all_to_all x1, waiting for transfers between devices, local(): lax.all_to_all(stored, 'vol', split_axis=2, concat_axis=0, tiled=True)  28.7 us
    ppermute x3, waiting for transfers between devices, extended_2(): after = lax.ppermute(first, axis, down)  21.6 us
    ppermute x3, starting transfers between devices, extended_2(): before = lax.ppermute(last, axis, up)  14.9 us
    all_to_all x1, starting transfers between devices, local(): lax.all_to_all(stored, 'vol', split_axis=2, concat_axis=0, tiled=True)  14.3 us
    ppermute x3, starting transfers between devices, extended_2(): after = lax.ppermute(first, axis, down)  8.16 us
    add x2, other arithmetic, advance(): return center + 0.2 * total  5.34 us
    convert_element_type x1, other arithmetic, local(): stored = field.astype(jnp.bfloat16)  2.7 us
  transfers between devices with their start and end apart: 7, of which 4 were waited for; matrix products, arithmetic and copies ran while one was open for 1% of the time, Pallas kernels for 0%

commit v1 on v0

--- a/solution.py
+++ b/solution.py
@@ -5,6 +5,13 @@
 
 PASSES = 3
 BAND = 16
+
+
+def trade_parts(x, name, split, join):
+    size = lax.axis_size(name)
+    pieces = jnp.stack(jnp.split(x, size, axis=split), axis=0)
+    pieces = lax.all_to_all(pieces, name, split_axis=0, concat_axis=0)
+    return jnp.concatenate(pieces, axis=join)
 
 
 def extended_2(value, sides, width):
@@ -65,7 +72,7 @@
         extended = extended_2(field, (("strip", 2),), 1)
         field = advance(extended, kap)
     stored = field.astype(jnp.bfloat16)
-    ratio, slope = detrend(lax.all_to_all(stored, "vol", split_axis=2, concat_axis=0, tiled=True))
+    ratio, slope = detrend(trade_parts(stored, "vol", 2, 0))
     return (ratio[:, :, :, None, :], slope[:, :, :, None, :])
 
 

time: 107 us -> 146 us (1.36)
  local copies, waits for them, and re-layouts: 7.04 us -> 43.7 us
  other arithmetic: 10.3 us -> 12.9 us
    unnamed x5 -> x68, local copies, waits for them, and re-layouts: 0.39 us -> 39 us
    convert_element_type x1 -> x2, other arithmetic: 2.7 us -> 5.4 us  [local(): stored = field.astype(jnp.bfloat16)]
    convert_element_type x1 -> x0, local copies, waits for them, and re-layouts: 2.05 us -> none  [local(): stored = field.astype(jnp.bfloat16)]
where the time goes in v1:
time: 146 us
  waiting for transfers between devices  50.3 us (34%)
  local copies, waits for them, and re-layouts  43.7 us (30%)
  starting transfers between devices  37.3 us (26%)
  other arithmetic  12.9 us (9%)
    unnamed x68, local copies, waits for them, and re-layouts  39 us
    all_to_all x1, waiting for transfers between devices, trade_parts(): pieces = lax.all_to_all(pieces, name, split_axis=0, concat_axis=0)  28.7 us
    ppermute x3, waiting for transfers between devices, extended_2(): after = lax.ppermute(first, axis, down)  21.6 us
    ppermute x3, starting transfers between devices, extended_2(): before = lax.ppermute(last, axis, up)  14.9 us
    all_to_all x1, starting transfers between devices, trade_parts(): pieces = lax.all_to_all(pieces, name, split_axis=0, concat_axis=0)  14.3 us
    ppermute x3, starting transfers between devices, extended_2(): after = lax.ppermute(first, axis, down)  8.15 us
    convert_element_type x2, other arithmetic, local(): stored = field.astype(jnp.bfloat16)  5.4 us
    add x2, other arithmetic, advance(): return center + 0.2 * total  5.32 us
  transfers between devices with their start and end apart: 7, of which 4 were waited for; matrix products, arithmetic and copies ran while one was open for 1% of the time, Pallas kernels for 0%

profile of v1, /device:TPU:7, one launch (start us, length us, event | category | flops | bytes accessed | tf_op | source)
XLA Modules:
  0.0 145.8 jit_solution(15673283931357798835)
XLA Ops:
  0.7 0.9 fusion.23
  1.5 10.6 %collective-permute-start = (f32[2,1,1,1024]{3,2,1,0:T(1,128)S(1)}, f32[2,1,1,1024]{3,2,1,0:T(1,128)S(1)}, u32[]{:S(2)}, u32[]{:S(2)}) collective-permute-start(f32[2,1,1,1024]{3,2,1,0:T(1,128)S(1)} %get-tuple-element.12), channel_id=1, source_target_pairs={{0,1},{1,2},{2,3},{3,4},{4,5},{5,6},{6,7},{8,9},{9,10},{10,11},{11... | collective-permute-start | bytes 24584 | tf_op jit(solution)/shard_map/ppermute | solution.py:24
  12.1 1.9 %collective-permute-start.1 = (f32[2,1,1,1024]{3,2,1,0:T(1,128)S(1)}, f32[2,1,1,1024]{3,2,1,0:T(1,128)S(1)}, u32[]{:S(2)}, u32[]{:S(2)}) collective-permute-start(f32[2,1,1,1024]{3,2,1,0:T(1,128)S(1)} %get-tuple-element.13), channel_id=1, source_target_pairs={{1,0},{2,1},{3,2},{4,3},{5,4},{6,5},{7,6},{9,8},{10,9},{11,10},{12... | collective-permute-start | bytes 24584 | tf_op jit(solution)/shard_map/ppermute | solution.py:25
  14.0 1.5 %convert_element_type.49 = f32[2,1,256,1024]{3,2,1,0:T(8,128)S(1)} convert(bf16[2,1,256,1024]{3,2,1,0:T(8,128)(2,1)} %param.2) | non-fusion elementwise | flops 524288 | bytes 3145728 | tf_op jit(solution)/shard_map/convert_element_type | solution.py:70
  15.5 7.0 %collective-permute-done.1 = f32[2,1,1,1024]{3,2,1,0:T(1,128)S(1)} collective-permute-done((f32[2,1,1,1024]{3,2,1,0:T(1,128)S(1)}, f32[2,1,1,1024]{3,2,1,0:T(1,128)S(1)}, u32[]{:S(2)}, u32[]{:S(2)}) %collective-permute-start.1) | collective-permute-done | bytes 8224 | tf_op jit(solution)/shard_map/ppermute | solution.py:25
  22.5 2.7 %convert_add_fusion = f32[2,1,256,1024]{3,2,1,0:T(8,128)S(1)} fusion(bf16[2,1,256,1024]{3,2,1,0:T(8,128)(2,1)S(1)} %copy-done, f32[2,1,256,1024]{3,2,1,0:T(8,128)S(1)} %convert_element_type.49, f32[2,1,1,1024]{3,2,1,0:T(1,128)S(1)} %collective-permute-done.1, f32[2,1,1,1024]{3,2,1,0:T(1,128)S(1)} %collective-permute-done, f32[2]{0:T(128)S(1)} %copy-done.1), kind=kLoop, calls=%fused_computation | loop fusion | flops 14680064 | bytes 5259272 | tf_op jit(solution)/shard_map/add | solution.py:43
  25.2 2.4 %collective-permute-start.2 = (f32[2,1,1,1024]{3,2,1,0:T(1,128)S(1)}, f32[2,1,1,1024]{3,2,1,0:T(1,128)S(1)}, u32[]{:S(2)}, u32[]{:S(2)}) collective-permute-start(f32[2,1,1,1024]{3,2,1,0:T(1,128)S(1)} %get-tuple-element.10), channel_id=1, source_target_pairs={{0,1},{1,2},{2,3},{3,4},{4,5},{5,6},{6,7},{8,9},{9,10},{10,11},{11... | collective-permute-start | bytes 24584 | tf_op jit(solution)/shard_map/ppermute | solution.py:24
  27.6 2.9 %collective-permute-start.3 = (f32[2,1,1,1024]{3,2,1,0:T(1,128)S(1)}, f32[2,1,1,1024]{3,2,1,0:T(1,128)S(1)}, u32[]{:S(2)}, u32[]{:S(2)}) collective-permute-start(f32[2,1,1,1024]{3,2,1,0:T(1,128)S(1)} %get-tuple-element.11), channel_id=1, source_target_pairs={{1,0},{2,1},{3,2},{4,3},{5,4},{6,5},{7,6},{9,8},{10,9},{11,10},{12... | collective-permute-start | bytes 24584 | tf_op jit(solution)/shard_map/ppermute | solution.py:25
  30.5 7.5 %collective-permute-done.3 = f32[2,1,1,1024]{3,2,1,0:T(1,128)S(1)} collective-permute-done((f32[2,1,1,1024]{3,2,1,0:T(1,128)S(1)}, f32[2,1,1,1024]{3,2,1,0:T(1,128)S(1)}, u32[]{:S(2)}, u32[]{:S(2)}) %collective-permute-start.3) | collective-permute-done | bytes 8224 | tf_op jit(solution)/shard_map/ppermute | solution.py:25
  38.1 2.6 %multiply_add_fusion = f32[2,1,256,1024]{3,2,1,0:T(8,128)S(1)} fusion(f32[2,1,256,1024]{3,2,1,0:T(8,128)S(1)} %convert_add_fusion, f32[2,1,1,1024]{3,2,1,0:T(1,128)S(1)} %collective-permute-done.3, f32[2,1,1,1024]{3,2,1,0:T(1,128)S(1)} %collective-permute-done.2, f32[2]{0:T(128)S(1)} %copy-done.1), kind=kLoop, calls=%fused_computation.30 | loop fusion | flops 14155776 | bytes 4210696 | tf_op jit(solution)/shard_map/add | solution.py:43
  40.7 1.9 %collective-permute-start.4 = (f32[2,1,1,1024]{3,2,1,0:T(1,128)S(1)}, f32[2,1,1,1024]{3,2,1,0:T(1,128)S(1)}, u32[]{:S(2)}, u32[]{:S(2)}) collective-permute-start(f32[2,1,1,1024]{3,2,1,0:T(1,128)S(1)} %get-tuple-element.8), channel_id=1, source_target_pairs={{0,1},{1,2},{2,3},{3,4},{4,5},{5,6},{6,7},{8,9},{9,10},{10,11},{11... | collective-permute-start | bytes 24584 | tf_op jit(solution)/shard_map/ppermute | solution.py:24
  42.7 3.4 %collective-permute-start.5 = (f32[2,1,1,1024]{3,2,1,0:T(1,128)S(1)}, f32[2,1,1,1024]{3,2,1,0:T(1,128)S(1)}, u32[]{:S(2)}, u32[]{:S(2)}) collective-permute-start(f32[2,1,1,1024]{3,2,1,0:T(1,128)S(1)} %get-tuple-element.9), channel_id=1, source_target_pairs={{1,0},{2,1},{3,2},{4,3},{5,4},{6,5},{7,6},{9,8},{10,9},{11,10},{12... | collective-permute-start | bytes 24584 | tf_op jit(solution)/shard_map/ppermute | solution.py:25
  46.0 7.0 %collective-permute-done.5 = f32[2,1,1,1024]{3,2,1,0:T(1,128)S(1)} collective-permute-done((f32[2,1,1,1024]{3,2,1,0:T(1,128)S(1)}, f32[2,1,1,1024]{3,2,1,0:T(1,128)S(1)}, u32[]{:S(2)}, u32[]{:S(2)}) %collective-permute-start.5) | collective-permute-done | bytes 8224 | tf_op jit(solution)/shard_map/ppermute | solution.py:25
  53.1 2.7 %fusion.26 = bf16[2,1,256,1024]{3,2,0,1:T(8,128)(2,1)S(1)} fusion(f32[2,1,256,1024]{3,2,1,0:T(8,128)S(1)} %multiply_add_fusion, f32[2,1,1,1024]{3,2,1,0:T(1,128)S(1)} %collective-permute-done.5, f32[2]{0:T(128)S(1)} %copy-done.1, f32[2,1,1,1024]{3,2,1,0:T(1,128)S(1)} %collective-permute-done.4), kind=kLoop, calls=%fused_computation.181 | loop fusion | flops 14680064 | bytes 3162120 | tf_op jit(solution)/shard_map/convert_element_type | solution.py:74
  56.4 0.6 constant_dynamic-update-slice_fusion.62
  57.6 0.6 constant_dynamic-update-slice_fusion.60
  58.8 0.6 constant_dynamic-update-slice_fusion.58
  60.1 0.6 constant_dynamic-update-slice_fusion.56
  61.3 0.6 constant_dynamic-update-slice_fusion.54
  62.5 0.6 constant_dynamic-update-slice_fusion.52
  63.8 0.6 constant_dynamic-update-slice_fusion.50
  65.0 0.6 constant_dynamic-update-slice_fusion.48
  66.2 0.6 constant_dynamic-update-slice_fusion.46
  67.4 0.6 constant_dynamic-update-slice_fusion.44
  68.7 0.6 constant_dynamic-update-slice_fusion.42
  69.9 0.6 constant_dynamic-update-slice_fusion.40
  71.1 0.6 constant_dynamic-update-slice_fusion.38
  72.4 0.6 constant_dynamic-update-slice_fusion.36
  73.6 0.6 constant_dynamic-update-slice_fusion.34
  74.8 0.6 constant_dynamic-update-slice_fusion.32
  76.0 0.6 constant_dynamic-update-slice_fusion.30
  77.3 0.6 constant_dynamic-update-slice_fusion.28
  78.5 0.6 constant_dynamic-update-slice_fusion.26
  79.7 0.6 constant_dynamic-update-slice_fusion.24
  81.0 0.6 constant_dynamic-update-slice_fusion.22
  82.2 0.6 constant_dynamic-update-slice_fusion.20
  83.4 0.6 constant_dynamic-update-slice_fusion.18
  84.6 0.6 constant_dynamic-update-slice_fusion.16
  85.9 0.6 constant_dynamic-update-slice_fusion.14
  87.1 0.6 constant_dynamic-update-slice_fusion.12
  88.3 0.6 constant_dynamic-update-slice_fusion.10
  94.5 2.7 %add_convert_fusion = bf16[2,1,256,1024]{3,2,1,0:T(8,128)(2,1)S(1)} fusion(f32[2,1,256,1024]{3,2,1,0:T(8,128)S(1)} %multiply_add_fusion, f32[2,1,1,1024]{3,2,1,0:T(1,128)S(1)} %collective-permute-done.5, f32[2,1,1,1024]{3,2,1,0:T(1,128)S(1)} %collective-permute-done.4, f32[2]{0:T(128)S(1)} %copy-done.1), kind=kLoop, calls=%fused_computation.29 | loop fusion | flops 14680064 | bytes 3162120 | tf_op jit(solution)/shard_map/convert_element_type | solution.py:74
  97.2 0.6 constant_dynamic-update-slice_fusion
  97.8 14.3 %all-to-all-start = ((bf16[64,2,1,4,1024]{4,3,1,2,0:T(4,128)(2,1)}), bf16[64,2,1,4,1024]{4,3,1,2,0:T(4,128)(2,1)S(1)}, u32[]{:S(2)}, u32[]{:S(2)}) async-start(bf16[64,2,1,4,1024]{4,3,1,2,0:T(4,128)(2,1)} %constant_dynamic-update-slice_fusion), calls=%async_computation | async-start | bytes 2097152 | tf_op jit(solution)/shard_map/all_to_all | solution.py:13
  112.2 28.7 %all-to-all-done = bf16[64,2,1,4,1024]{4,3,1,2,0:T(4,128)(2,1)S(1)} async-done(((bf16[64,2,1,4,1024]{4,3,1,2,0:T(4,128)(2,1)}), bf16[64,2,1,4,1024]{4,3,1,2,0:T(4,128)(2,1)S(1)}, u32[]{:S(2)}, u32[]{:S(2)}) %all-to-all-start) | async-done | bytes 1048608 | tf_op jit(solution)/shard_map/all_to_all | solution.py:13
  141.3 0.6 fusion.24
  142.3 1.6 %convert_element_type.55 = bf16[128,1,4,1,1024]{4,2,0,3,1:T(4,128)(2,1)} reshape(bf16[128,4096]{1,0:T(8,128)(2,1)S(1)} %get-tuple-element.14) | data formatting | bytes 2097152 | tf_op jit(solution)/shard_map/convert_element_type | solution.py:63
  144.2 1.6 %convert_element_type.56 = bf16[128,1,4,1,1024]{4,2,0,3,1:T(4,128)(2,1)} reshape(bf16[128,4096]{1,0:T(8,128)(2,1)S(1)} %pad_maximum_fusion.6) | data formatting | bytes 2097152 | tf_op jit(solution)/shard_map/convert_element_type | solution.py:64
  (50 shorter events, 23.2 us)
Async XLA Ops:
  0.6 21.9 %copy-start = (bf16[2,1,256,1024]{3,2,1,0:T(8,128)(2,1)S(1)}, bf16[2,1,256,1024]{3,2,1,0:T(8,128)(2,1)}, u32[]{:S(2)}) copy-start(bf16[2,1,256,1024]{3,2,1,0:T(8,128)(2,1)} %param.2) | copy-start | bytes 3145732
  0.6 21.9 %copy-start.1 = (f32[2]{0:T(128)S(1)}, f32[2]{0:T(128)}, u32[]{:S(2)}) copy-start(f32[2]{0:T(128)} %param.3) | copy-start | bytes 28
  1.5 14.0 %collective-permute-start = (f32[2,1,1,1024]{3,2,1,0:T(1,128)S(1)}, f32[2,1,1,1024]{3,2,1,0:T(1,128)S(1)}, u32[]{:S(2)}, u32[]{:S(2)}) collective-permute-start(f32[2,1,1,1024]{3,2,1,0:T(1,128)S(1)} %get-tuple-element.12), channel_id=1, source_target_pairs={{0,1},{1,2},{2,3},{3,4},{4,5},{5,6},{6,7},{8,9},{9,10},{10,11},{11... | collective-permute-start | bytes 24584 | tf_op jit(solution)/shard_map/ppermute | solution.py:24
  12.1 10.4 %collective-permute-start.1 = (f32[2,1,1,1024]{3,2,1,0:T(1,128)S(1)}, f32[2,1,1,1024]{3,2,1,0:T(1,128)S(1)}, u32[]{:S(2)}, u32[]{:S(2)}) collective-permute-start(f32[2,1,1,1024]{3,2,1,0:T(1,128)S(1)} %get-tuple-element.13), channel_id=1, source_target_pairs={{1,0},{2,1},{3,2},{4,3},{5,4},{6,5},{7,6},{9,8},{10,9},{11,10},{12... | collective-permute-start | bytes 24584 | tf_op jit(solution)/shard_map/ppermute | solution.py:25
  25.2 5.3 %collective-permute-start.2 = (f32[2,1,1,1024]{3,2,1,0:T(1,128)S(1)}, f32[2,1,1,1024]{3,2,1,0:T(1,128)S(1)}, u32[]{:S(2)}, u32[]{:S(2)}) collective-permute-start(f32[2,1,1,1024]{3,2,1,0:T(1,128)S(1)} %get-tuple-element.10), channel_id=1, source_target_pairs={{0,1},{1,2},{2,3},{3,4},{4,5},{5,6},{6,7},{8,9},{9,10},{10,11},{11... | collective-permute-start | bytes 24584 | tf_op jit(solution)/shard_map/ppermute | solution.py:24
  27.6 10.4 %collective-permute-start.3 = (f32[2,1,1,1024]{3,2,1,0:T(1,128)S(1)}, f32[2,1,1,1024]{3,2,1,0:T(1,128)S(1)}, u32[]{:S(2)}, u32[]{:S(2)}) collective-permute-start(f32[2,1,1,1024]{3,2,1,0:T(1,128)S(1)} %get-tuple-element.11), channel_id=1, source_target_pairs={{1,0},{2,1},{3,2},{4,3},{5,4},{6,5},{7,6},{9,8},{10,9},{11,10},{12... | collective-permute-start | bytes 24584 | tf_op jit(solution)/shard_map/ppermute | solution.py:25
  40.7 5.3 %collective-permute-start.4 = (f32[2,1,1,1024]{3,2,1,0:T(1,128)S(1)}, f32[2,1,1,1024]{3,2,1,0:T(1,128)S(1)}, u32[]{:S(2)}, u32[]{:S(2)}) collective-permute-start(f32[2,1,1,1024]{3,2,1,0:T(1,128)S(1)} %get-tuple-element.8), channel_id=1, source_target_pairs={{0,1},{1,2},{2,3},{3,4},{4,5},{5,6},{6,7},{8,9},{9,10},{10,11},{11... | collective-permute-start | bytes 24584 | tf_op jit(solution)/shard_map/ppermute | solution.py:24
  42.7 10.4 %collective-permute-start.5 = (f32[2,1,1,1024]{3,2,1,0:T(1,128)S(1)}, f32[2,1,1,1024]{3,2,1,0:T(1,128)S(1)}, u32[]{:S(2)}, u32[]{:S(2)}) collective-permute-start(f32[2,1,1,1024]{3,2,1,0:T(1,128)S(1)} %get-tuple-element.9), channel_id=1, source_target_pairs={{1,0},{2,1},{3,2},{4,3},{5,4},{6,5},{7,6},{9,8},{10,9},{11,10},{12... | collective-permute-start | bytes 24584 | tf_op jit(solution)/shard_map/ppermute | solution.py:25
  97.8 43.1 %all-to-all-start = ((bf16[64,2,1,4,1024]{4,3,1,2,0:T(4,128)(2,1)}), bf16[64,2,1,4,1024]{4,3,1,2,0:T(4,128)(2,1)S(1)}, u32[]{:S(2)}, u32[]{:S(2)}) async-start(bf16[64,2,1,4,1024]{4,3,1,2,0:T(4,128)(2,1)} %constant_dynamic-update-slice_fusion), calls=%async_computation | async-start | bytes 2097152 | tf_op jit(solution)/shard_map/all_to_all | solution.py:13
